TPU v7x, 512 devices: a whole 4x4x16 slice. The times are simulated.
512 devices in a mesh: leaf: 128 (over x, z, core), sub: 4 (over y).
Axes of the slice: x: 4, y: 4, z: 16, core: 2. Of those that a mesh axis runs over, the one named last changes fastest.
Arguments:
- probe_rhs: float32 [32, 524288], P(None, ('leaf', 'sub')), may hold values from -22.5 to 22.5
- coords: float32 [3, 524288], P(None, ('leaf', 'sub')), may hold values from -820.7 to 820.7
- near_list: int32 [2048, 5], P(('leaf', 'sub')), may hold values from -1 to 2047, as said below
- far_leaf_list: int32 [2048, 8], P(('leaf', 'sub')), may hold values from -1 to 2047, as said below
- far_group_list: int32 [128, 16], P('leaf'), may hold values from -1 to 127, as said below
- leaf_basis: float32 [2048, 64, 256], P(('leaf', 'sub')), may hold values from -0.375 to 0.375
- leaf_skeleton: float32 [3, 131072], P(None, ('leaf', 'sub')), may hold values from -820.7 to 820.7
- leaf_transfer: float32 [2048, 64, 64], P(('leaf', 'sub')), may hold values from -0.375 to 0.375
- device_transfer: float32 [512, 64, 64], P(('leaf', 'sub')), may hold values from -0.375 to 0.375
- group_skeleton: float32 [3, 8192], P(None, 'leaf'), may hold values from -1.5 to 4.5
Outputs:
- solution: float32 [32, 524288], P(None, ('leaf', 'sub'))
- residual: float32 [32, 524288], P(None, ('leaf', 'sub'))
Inputs may be any that keep to these rules, and one draw needn't show every extreme that they name: `near_list`: row i names distinct leaves within 2 of i, always i itself, -1 in unused slots, in any order; j is named in row i exactly when i is named in row j. `far_leaf_list`: row i names distinct leaves of the same group of 16 consecutive leaves, each more than 2 away from i, -1 in unused slots, in any order; the relation is symmetric. `far_group_list`: row g names distinct groups other than g, -1 in unused slots, in any order; the relation is symmetric.
All inputs are finite; a program needn't handle non-finite values.
Results may differ from a plain program's by a relative error of at most 0.0003.
Values sent between devices are 32-bit elements; how exact they have to be, the bound alone decides.
A program may use at most 64 MiB of HBM per device.

v0:
```python
import jax
import jax.numpy as jnp
from jax import lax
from jax.sharding import Mesh
from jax.sharding import PartitionSpec as P

LEAF = 256
RANK = 64
PROBES = 32
REACH = 2
ITERS = 2
LEAF_SUB = ("leaf_0", "leaf_1", "leaf_2", "sub")
LEAF_AXES = ("leaf_0", "leaf_1", "leaf_2")


NOISE = 1.0
ROOT_FIVE = 5.0**0.5
HIGHEST = lax.Precision.HIGHEST


def copy_for_each(shard, axis):
    count = lax.axis_size(axis)
    return lax.all_to_all(
        jnp.broadcast_to(shard[None], (count, *shard.shape)), axis, 0, 0, tiled=True
    )


def over_copies(shard, axis):
    return copy_for_each(shard, axis).sum(axis=0)


def over_axes(shard, axes):
    far, near = axes
    nearer = over_copies(shard, near)
    return over_copies(nearer, far)


def padded(shard, sides, width):
    edges = {}
    for axis, dim in sides:
        count, length = (lax.axis_size(axis), shard.shape[dim])
        up = [(i, (i + 1) % count) for i in range(count - 1)]
        last = lax.slice_in_dim(shard, length - width, length, axis=dim)
        first = lax.slice_in_dim(shard, 0, width, axis=dim)
        edges[dim] = (
            lax.ppermute(last, axis, up),
            lax.ppermute(first, axis, [(b, a) for a, b in up]),
        )
    done = []
    for _, dim in sides:
        low, high = edges[dim]
        around = [(width, width) if d in done else (0, 0) for d in range(shard.ndim)]
        shard = jnp.concatenate([jnp.pad(low, around), shard, jnp.pad(high, around)], axis=dim)
        done.append(dim)
    return shard


def in_order(tiles, dim):
    shape = list(tiles.shape[1:])
    shape[dim] *= tiles.shape[0]
    return jnp.moveaxis(tiles, 0, dim).reshape(shape)


def collect(shard, axis, dim):
    return in_order(copy_for_each(shard, axis), dim)


def whole_of(shard, axes, dim):
    far, near = axes
    tiles = copy_for_each(copy_for_each(shard, far), near)
    return in_order(tiles.swapaxes(0, 1).reshape(-1, *shard.shape), dim)


def matern(left_points, right_points):
    spread = left_points[..., :, :, None] - right_points[..., :, None, :]
    scaled = ROOT_FIVE * jnp.sqrt(jnp.sum(spread * spread, axis=-3))
    return (1.0 + scaled + scaled * scaled / 3.0) * jnp.exp(-scaled)


def near_field(padded_vec, padded_pts, weights):
    local_leaves = weights.shape[0]
    window = weights.shape[1]
    padded_count = local_leaves + window - 1
    vec_blocks = padded_vec.reshape(PROBES, padded_count, LEAF)
    pts_blocks = padded_pts.reshape(3, padded_count, LEAF)
    padded_weights = jnp.pad(weights, ((REACH, REACH), (0, 0)))

    def one_position(position):
        own_points = lax.dynamic_index_in_dim(pts_blocks, position, 1, keepdims=False)
        own_values = lax.dynamic_index_in_dim(vec_blocks, position, 1, keepdims=False)
        own_weights = lax.dynamic_index_in_dim(padded_weights, position, 0, keepdims=False)
        forward = jnp.zeros((PROBES, LEAF), jnp.float32)
        backward = []
        for offset in range(REACH + 1):
            other_points = lax.dynamic_index_in_dim(
                pts_blocks, position + offset, 1, keepdims=False
            )
            kernel_tile = matern(own_points, other_points)
            other_values = lax.dynamic_index_in_dim(
                vec_blocks, position + offset, 1, keepdims=False
            )
            forward = forward + own_weights[REACH + offset] * jnp.dot(
                other_values, kernel_tile.T, precision=HIGHEST
            )
            if offset > 0:
                other_weights = lax.dynamic_index_in_dim(
                    padded_weights, position + offset, 0, keepdims=False
                )
                backward.append(
                    other_weights[REACH - offset]
                    * jnp.dot(own_values, kernel_tile, precision=HIGHEST)
                )
        return (forward, jnp.stack(backward, axis=0))

    forward_all, backward_all = lax.map(
        one_position, jnp.arange(local_leaves + REACH, dtype=jnp.int32)
    )
    totals = forward_all[REACH : REACH + local_leaves]
    for offset in range(1, REACH + 1):
        totals = totals + backward_all[REACH - offset : REACH - offset + local_leaves, offset - 1]
    return totals


def squares(residual):
    return over_axes(
        jnp.sum(residual * residual, axis=1), (("leaf_0", "leaf_1"), ("leaf_2", "sub"))
    )


def shards(
    probe_rhs,
    coords,
    near_list,
    far_leaf_list,
    far_group_list,
    leaf_basis,
    leaf_skeleton,
    leaf_transfer,
    device_transfer,
    group_skeleton,
):
    local_leaves = near_list.shape[0]
    window = 2 * REACH + 1
    first_leaf = lax.axis_index(LEAF_SUB) * local_leaves
    group_first = lax.axis_index(LEAF_AXES) * local_leaves * lax.axis_size("sub")
    targets = (
        first_leaf
        + jnp.arange(local_leaves, dtype=jnp.int32)[:, None, None]
        + jnp.arange(window, dtype=jnp.int32)[None, None, :]
        - REACH
    )
    near_weights = jnp.sum((near_list[:, :, None] == targets).astype(jnp.float32), axis=1)
    padded_pts = padded(coords, ((LEAF_SUB, 1),), REACH * LEAF)
    group_skel = collect(leaf_skeleton, "sub", 1).reshape(3, -1, RANK)
    own_skel = jnp.transpose(leaf_skeleton.reshape(3, local_leaves, RANK), (1, 0, 2))
    partner_local = far_leaf_list - group_first
    partner_skel = jnp.take(group_skel, jnp.maximum(partner_local, 0), axis=1)
    partner_skel = jnp.transpose(partner_skel, (1, 2, 0, 3))
    leaf_tiles = (
        matern(own_skel[:, None], partner_skel)
        * (far_leaf_list >= 0).astype(jnp.float32)[:, :, None, None]
    )
    every_group = whole_of(group_skeleton, (("leaf_0", "leaf_1"), "leaf_2"), 1).reshape(3, -1, RANK)
    group_list = far_group_list[0]
    partner_groups = jnp.transpose(
        jnp.take(every_group, jnp.maximum(group_list, 0), axis=1), (1, 0, 2)
    )
    group_tiles = (
        matern(group_skeleton[None], partner_groups)
        * (group_list >= 0).astype(jnp.float32)[:, None, None]
    )
    slots_group = group_list.shape[0]
    solution = jnp.zeros_like(probe_rhs)
    residual = probe_rhs
    direction = probe_rhs
    norm_now = squares(residual)
    for iteration in range(ITERS):
        padded_vec = padded(direction, ((LEAF_SUB, 1),), REACH * LEAF)
        near_part = near_field(padded_vec, padded_pts, near_weights)
        by_leaf = direction.reshape(PROBES, local_leaves, LEAF)
        coefficients = jnp.einsum("pla,lra->lrp", by_leaf, leaf_basis, precision=HIGHEST)
        add_piece = collect(coefficients.reshape(local_leaves, RANK * PROBES), "sub", 0)
        add_count = add_piece.shape[0]
        add_chosen = (
            partner_local[:, :, None] == jnp.arange(add_count, dtype=jnp.int32)[None, None, :]
        ).astype(jnp.float32)
        picked = jnp.einsum("lkm,mx->lkx", add_chosen, add_piece, precision=HIGHEST).reshape(
            local_leaves, -1, RANK, PROBES
        )
        leaf_far = jnp.zeros((local_leaves, RANK, PROBES), jnp.float32) + jnp.einsum(
            "lkrs,lksp->lrp", leaf_tiles, picked, precision=HIGHEST
        )
        device_coef = jnp.einsum("lrs,lrp->sp", leaf_transfer, coefficients, precision=HIGHEST)
        group_term = jnp.dot(device_transfer[0].T, device_coef, precision=HIGHEST).T
        summed = over_copies(group_term.reshape(1, PROBES * RANK), "sub")
        piece = whole_of(summed, (("leaf_0", "leaf_1"), "leaf_2"), 0)
        count = piece.shape[0]
        chosen = (group_list[:, None] == jnp.arange(count, dtype=jnp.int32)[None, :]).astype(
            jnp.float32
        )
        apply_picked = jnp.zeros((slots_group, PROBES * RANK), jnp.float32) + jnp.dot(
            chosen, piece, precision=HIGHEST
        )
        group_far = jnp.einsum(
            "krs,kps->rp",
            group_tiles,
            apply_picked.reshape(slots_group, PROBES, RANK),
            precision=HIGHEST,
        )
        device_far = jnp.dot(device_transfer[0], group_far, precision=HIGHEST)
        leaf_total = leaf_far + jnp.einsum(
            "lrs,sp->lrp", leaf_transfer, device_far, precision=HIGHEST
        )
        far_part = jnp.einsum("lra,lrp->pla", leaf_basis, leaf_total, precision=HIGHEST)
        near_flat = jnp.transpose(near_part, (1, 0, 2)).reshape(PROBES, -1)
        image_vec = NOISE * direction + near_flat + far_part.reshape(PROBES, -1)
        curvature = over_axes(
            jnp.sum(direction * image_vec, axis=1), (("leaf_0", "leaf_1"), ("leaf_2", "sub"))
        )
        step_length = norm_now / curvature
        solution = solution + step_length[:, None] * direction
        residual = residual - step_length[:, None] * image_vec
        if iteration + 1 < ITERS:
            norm_next = squares(residual)
            direction = residual + (norm_next / norm_now)[:, None] * direction
            norm_now = norm_next
    return (solution, residual)


def solution(mesh):
    finer = Mesh(
        mesh.devices.reshape(4, 16, 2, mesh.shape["sub"]), ("leaf_0", "leaf_1", "leaf_2", "sub")
    )
    in_specs = (
        P(None, LEAF_SUB),
        P(None, LEAF_SUB),
        P(LEAF_SUB, None),
        P(LEAF_SUB, None),
        P(LEAF_AXES, None),
        P(LEAF_SUB, None, None),
        P(None, LEAF_SUB),
        P(LEAF_SUB, None, None),
        P(LEAF_SUB, None, None),
        P(None, LEAF_AXES),
    )
    out_specs = (P(None, LEAF_SUB), P(None, LEAF_SUB))
    return jax.shard_map(
        shards, mesh=finer, in_specs=in_specs, out_specs=out_specs, check_vma=False
    )
```

profile of v0, /device:TPU:1, one launch (start us, length us, event | category | flops | bytes accessed | tf_op | source)
XLA Modules:
  0.0 422.2 jit_solution(17051980069671088770)
XLA Ops:
  0.7 1.3 broadcast_in_dim.113
  2.0 5.0 %all-to-all-start.2 = ((f32[4,3,256]{2,1,0:T(4,128)}), f32[4,3,256]{2,1,0:T(4,128)S(1)}, u32[]{:S(2)}, u32[]{:S(2)}) async-start(f32[4,3,256]{2,1,0:T(4,128)} %broadcast_in_dim.113), calls=%async_computation.2 | async-start | bytes 32768 | tf_op jit(solution)/shard_map/all_to_all | solution.py:23
  7.9 9.8 %collective-permute-start.1 = (f32[32,512]{1,0:T(8,128)S(1)}, f32[32,512]{1,0:T(8,128)S(1)}, u32[]{:S(2)}, u32[]{:S(2)}) collective-permute-start(f32[32,512]{1,0:T(8,128)S(1)} %get-tuple-element.257), channel_id=1, source_target_pairs={{1,0},{2,1},{3,2},{4,3},{5,4},{6,5},{7,6},{8,7},{9,8},{10,9},{11,1... | collective-permute-start | bytes 196616 | tf_op jit(solution)/shard_map/ppermute | solution.py:47
  17.8 1.9 collective-permute-start
  20.4 4.8 %collective-permute-start.3 = (f32[3,512]{1,0:T(4,128)S(1)}, f32[3,512]{1,0:T(4,128)S(1)}, u32[]{:S(2)}, u32[]{:S(2)}) collective-permute-start(f32[3,512]{1,0:T(4,128)S(1)} %get-tuple-element.259), channel_id=1, source_target_pairs={{1,0},{2,1},{3,2},{4,3},{5,4},{6,5},{7,6},{8,7},{9,8},{10,9},{11,1... | collective-permute-start | bytes 18440 | tf_op jit(solution)/shard_map/ppermute | solution.py:47
  25.3 1.9 collective-permute-start.2
  30.2 1.3 fusion.100
  31.4 1.1 convolution_bitcast_fusion.12
  34.7 3.3 all-to-all-start.6
  39.3 2.9 all-to-all-done.6
  42.2 16.9 %all-to-all-start.4 = ((f32[64,1,192]{2,1,0:T(1,128)}), f32[64,1,192]{2,1,0:T(1,128)S(1)}, u32[]{:S(2)}, u32[]{:S(2)}) async-start(f32[64,1,192]{2,1,0:T(1,128)} %reshape.276), calls=%async_computation.4 | async-start | bytes 131072 | tf_op jit(solution)/shard_map/all_to_all | solution.py:23
  59.3 13.3 %all-to-all-done.4 = f32[64,1,192]{2,1,0:T(1,128)S(1)} async-done(((f32[64,1,192]{2,1,0:T(1,128)}), f32[64,1,192]{2,1,0:T(1,128)S(1)}, u32[]{:S(2)}, u32[]{:S(2)}) %all-to-all-start.4) | async-done | bytes 49184 | tf_op jit(solution)/shard_map/all_to_all | solution.py:23
  73.3 3.3 all-to-all-start.3
  78.3 3.2 all-to-all-done.3
  81.4 6.2 %all_to_all.103 = f32[2,1,12288]{2,1,0:T(1,128)S(1)} all-to-all(f32[2,1,12288]{2,1,0:T(1,128)S(1)} %reshape.278), channel_id=1, replica_groups=mesh['leaf_0'=4,'leaf_1'=16,'leaf_2'=2,'sub'=4] {'leaf_2'}, dimensions={0} | all-to-all | bytes 196608 | tf_op jit(solution)/shard_map/all_to_all | solution.py:23
  87.7 1.1 broadcast_in_dim.124
  88.8 4.7 %all-to-all-start.7 = ((f32[64,1,2048]{2,1,0:T(1,128)}), f32[64,1,2048]{2,1,0:T(1,128)S(1)}, u32[]{:S(2)}, u32[]{:S(2)}) async-start(f32[64,1,2048]{2,1,0:T(1,128)} %broadcast_in_dim.124), calls=%async_computation.7 | async-start | bytes 1048576 | tf_op jit(solution)/shard_map/all_to_all | solution.py:23
  93.5 69.1 %while.28 = (s32[]{:T(128)}, f32[6,32,256]{2,1,0:T(8,128)S(1)}, f32[6,2,32,256]{3,2,1,0:T(8,128)S(1)}, s32[6]{0:T(128)S(1)}, f32[8,5]{1,0:T(8,128)S(1)}, /*index...) while((s32[]{:T(128)}, f32[6,32,256]{2,1,0:T(8,128)S(1)}, ...), condition=%wide.region_8.9_spmd, body=%wide.region_4.8_spmd.sunk | while | flops 129769488 | bytes 2846183 | solution.py:115
  100.8 1.1 fusion.197
  101.9 1.1 fusion.198
  111.2 1.1 convolution_multiply_fusion.12
  112.3 1.1 fusion.197
  113.4 1.1 fusion.198
  123.8 1.1 fusion.197
  124.9 1.1 fusion.198
  135.4 1.1 fusion.197
  136.5 1.1 fusion.198
  146.9 1.1 fusion.197
  148.0 1.1 fusion.198
  158.4 1.1 fusion.197
  159.5 1.1 fusion.198
  163.6 1.7 convolution_bitcast_fusion.3
  167.4 1.1 multiply_reduce_fusion.7
  168.8 4.9 %all_to_all.104 = f32[2,64,1,2048]{3,1,2,0:T(8,128)S(1)} all-to-all(f32[2,64,1,2048]{3,1,2,0:T(8,128)S(1)} %broadcast_in_dim.126), channel_id=1, replica_groups=mesh['leaf_0'=4,'leaf_1'=16,'leaf_2'=2,'sub'=4] {'leaf_2'}, dimensions={0} | all-to-all | bytes 2097152 | tf_op jit(solution)/shard_map/all_to_all | solution.py:23
  175.9 1.3 fusion.123
  179.2 7.2 %all_to_all.105 = f32[8,1,32]{2,1,0:T(1,128)S(1)} all-to-all(f32[8,1,32]{2,1,0:T(1,128)S(1)} %broadcast_in_dim.110), channel_id=1, replica_groups=mesh['leaf_0'=4,'leaf_1'=16,'leaf_2'=2,'sub'=4] {'leaf_2','sub'}, dimensions={0} | all-to-all | bytes 2048 | tf_op jit(solution)/shard_map/all_to_all | solution.py:23
  187.0 3.9 all-to-all-start.9
  190.9 4.5 %all-to-all-done.9 = f32[8,1,32]{2,1,0:T(1,128)S(1)} async-done(((f32[8,1,32]{2,1,0:T(1,128)}), f32[8,1,32]{2,1,0:T(1,128)S(1)}, u32[]{:S(2)}, u32[]{:S(2)}) %all-to-all-start.9) | async-done | bytes 1056 | tf_op jit(solution)/shard_map/all_to_all | solution.py:23
  196.0 14.8 %all-to-all-start.1 = ((f32[64,1,32]{2,1,0:T(1,128)}), f32[64,1,32]{2,1,0:T(1,128)S(1)}, u32[]{:S(2)}, u32[]{:S(2)}) async-start(f32[64,1,32]{2,1,0:T(1,128)} %broadcast_in_dim.111), calls=%async_computation.1 | async-start | bytes 65536 | tf_op jit(solution)/shard_map/all_to_all | solution.py:23
  210.9 13.2 %all-to-all-done.1 = f32[64,1,32]{2,1,0:T(1,128)S(1)} async-done(((f32[64,1,32]{2,1,0:T(1,128)}), f32[64,1,32]{2,1,0:T(1,128)S(1)}, u32[]{:S(2)}, u32[]{:S(2)}) %all-to-all-start.1) | async-done | bytes 8224 | tf_op jit(solution)/shard_map/all_to_all | solution.py:23
  224.7 4.6 %all-to-all-start.10 = ((f32[64,1,32]{2,1,0:T(1,128)}), f32[64,1,32]{2,1,0:T(1,128)S(1)}, u32[]{:S(2)}, u32[]{:S(2)}) async-start(f32[64,1,32]{2,1,0:T(1,128)} %broadcast_in_dim.128), calls=%async_computation.10 | async-start | bytes 65536 | tf_op jit(solution)/shard_map/all_to_all | solution.py:23
  229.4 13.1 %all-to-all-done.10 = f32[64,1,32]{2,1,0:T(1,128)S(1)} async-done(((f32[64,1,32]{2,1,0:T(1,128)}), f32[64,1,32]{2,1,0:T(1,128)S(1)}, u32[]{:S(2)}, u32[]{:S(2)}) %all-to-all-start.10) | async-done | bytes 8224 | tf_op jit(solution)/shard_map/all_to_all | solution.py:23
  242.8 10.2 %all_to_all.107 = f32[8,1,32]{2,1,0:T(1,128)S(1)} all-to-all(f32[8,1,32]{2,1,0:T(1,128)S(1)} %broadcast_in_dim.129), channel_id=1, replica_groups=mesh['leaf_0'=4,'leaf_1'=16,'leaf_2'=2,'sub'=4] {'leaf_2','sub'}, dimensions={0} | all-to-all | bytes 2048 | tf_op jit(solution)/shard_map/all_to_all | solution.py:23
  253.1 17.1 %all_to_all.108 = f32[64,1,32]{2,1,0:T(1,128)S(1)} all-to-all(f32[64,1,32]{2,1,0:T(1,128)S(1)} %broadcast_in_dim.220), channel_id=1, replica_groups=mesh['leaf_0'=4,'leaf_1'=16,'leaf_2'=2,'sub'=4] {'leaf_0','leaf_1'}, dimensions={0} | all-to-all | bytes 16384 | tf_op jit(solution)/shard_map/all_to_all | solution.py:23
  270.9 4.5 %collective-permute-start.5 = (f32[32,512]{1,0:T(8,128)S(1)}, f32[32,512]{1,0:T(8,128)S(1)}, u32[]{:S(2)}, u32[]{:S(2)}) collective-permute-start(f32[32,512]{1,0:T(8,128)S(1)} %get-tuple-element.255), channel_id=1, source_target_pairs={{1,0},{2,1},{3,2},{4,3},{5,4},{6,5},{7,6},{8,7},{9,8},{10,9},{11,1... | collective-permute-start | bytes 196616 | tf_op jit(solution)/shard_map/ppermute | solution.py:47
  275.5 1.9 collective-permute-start.4
  278.3 3.4 all-to-all-start.14
  281.9 4.1 all-to-all-done.14
  286.6 3.3 all-to-all-start.13
  290.1 4.6 %all-to-all-done.13 = f32[4,4,2048]{2,1,0:T(4,128)S(1)} async-done(((f32[4,4,2048]{2,1,0:T(4,128)}), f32[4,4,2048]{2,1,0:T(4,128)S(1)}, u32[]{:S(2)}, u32[]{:S(2)}) %all-to-all-start.13) | async-done | bytes 131104 | tf_op jit(solution)/shard_map/all_to_all | solution.py:23
  294.7 1.1 broadcast_in_dim.225
  295.8 6.2 %all-to-all-start.15 = ((f32[64,1,2048]{2,1,0:T(1,128)}), f32[64,1,2048]{2,1,0:T(1,128)S(1)}, u32[]{:S(2)}, u32[]{:S(2)}) async-start(f32[64,1,2048]{2,1,0:T(1,128)} %broadcast_in_dim.225), calls=%async_computation.15 | async-start | bytes 1048576 | tf_op jit(solution)/shard_map/all_to_all | solution.py:23
  302.1 68.6 %while.29 = (s32[]{:T(128)}, f32[6,32,256]{2,1,0:T(8,128)S(1)}, f32[6,2,32,256]{3,2,1,0:T(8,128)S(1)}, s32[6]{0:T(128)S(1)}, f32[8,5]{1,0:T(8,128)S(1)}, /*index...) while((s32[]{:T(128)}, f32[6,32,256]{2,1,0:T(8,128)S(1)}, ...), condition=%wide.region_22.23_spmd, body=%wide.region_18.22_spmd.sunk | while | flops 129769488 | bytes 2846183 | solution.py:115
  310.4 1.1 fusion.210
  321.8 1.1 fusion.210
  333.2 1.1 fusion.210
  344.7 1.1 fusion.210
  356.1 1.1 fusion.210
  367.6 1.1 fusion.210
  372.0 2.3 convolution_bitcast_fusion.2
  374.6 6.4 %all_to_all.106 = f32[2,64,1,2048]{3,1,2,0:T(8,128)S(1)} all-to-all(f32[2,64,1,2048]{3,1,2,0:T(8,128)S(1)} %broadcast_in_dim.227), channel_id=1, replica_groups=mesh['leaf_0'=4,'leaf_1'=16,'leaf_2'=2,'sub'=4] {'leaf_2'}, dimensions={0} | all-to-all | bytes 2097152 | tf_op jit(solution)/shard_map/all_to_all | solution.py:23
  383.0 1.3 fusion.121
  386.3 7.3 %all_to_all.109 = f32[8,1,32]{2,1,0:T(1,128)S(1)} all-to-all(f32[8,1,32]{2,1,0:T(1,128)S(1)} %broadcast_in_dim.228), channel_id=1, replica_groups=mesh['leaf_0'=4,'leaf_1'=16,'leaf_2'=2,'sub'=4] {'leaf_2','sub'}, dimensions={0} | all-to-all | bytes 2048 | tf_op jit(solution)/shard_map/all_to_all | solution.py:23
  393.6 27.7 %all_to_all.110 = f32[64,1,32]{2,1,0:T(1,128)S(1)} all-to-all(f32[64,1,32]{2,1,0:T(1,128)S(1)} %broadcast_in_dim.229), channel_id=1, replica_groups=mesh['leaf_0'=4,'leaf_1'=16,'leaf_2'=2,'sub'=4] {'leaf_0','leaf_1'}, dimensions={0} | all-to-all | bytes 16384 | tf_op jit(solution)/shard_map/all_to_all | solution.py:23
  (295 shorter events, 90.5 us)
Async XLA Ops:
  0.6 29.5 %copy-start = (f32[4,64,256]{2,1,0:T(8,128)S(1)}, f32[4,64,256]{2,1,0:T(8,128)}, u32[]{:S(2)}) copy-start(f32[4,64,256]{2,1,0:T(8,128)} %param.19) | copy-start | bytes 786436
  0.6 32.3 %copy-start.11 = (f32[3,256]{1,0:T(4,128)S(1)}, f32[3,256]{1,0:T(4,128)}, u32[]{:S(2)}) copy-start(f32[3,256]{1,0:T(4,128)} %param.20) | copy-start | bytes 9220
  0.7 33.4 %copy-start.10 = (f32[3,1024]{1,0:T(4,128)S(1)}, f32[3,1024]{1,0:T(4,128)}, u32[]{:S(2)}) copy-start(f32[3,1024]{1,0:T(4,128)} %param.15) | copy-start | bytes 36868
  0.7 31.9 %copy-start.7 = (f32[1,64,64]{2,1,0:T(8,128)S(1)}, f32[1,64,64]{2,1,0:T(8,128)}, u32[]{:S(2)}) copy-start(f32[1,64,64]{2,1,0:T(8,128)} %param.22) | copy-start | bytes 49156
  0.7 32.5 %copy-start.12 = (f32[3,64]{1,0:T(4,128)S(1)}, f32[3,64]{1,0:T(4,128)}, u32[]{:S(2)}) copy-start(f32[3,64]{1,0:T(4,128)} %param.23) | copy-start | bytes 2308
  2.0 32.0 %all-to-all-start.2 = ((f32[4,3,256]{2,1,0:T(4,128)}), f32[4,3,256]{2,1,0:T(4,128)S(1)}, u32[]{:S(2)}, u32[]{:S(2)}) async-start(f32[4,3,256]{2,1,0:T(4,128)} %broadcast_in_dim.113), calls=%async_computation.2 | async-start | bytes 32768 | tf_op jit(solution)/shard_map/all_to_all | solution.py:23
  7.9 51.3 %collective-permute-start.1 = (f32[32,512]{1,0:T(8,128)S(1)}, f32[32,512]{1,0:T(8,128)S(1)}, u32[]{:S(2)}, u32[]{:S(2)}) collective-permute-start(f32[32,512]{1,0:T(8,128)S(1)} %get-tuple-element.257), channel_id=1, source_target_pairs={{1,0},{2,1},{3,2},{4,3},{5,4},{6,5},{7,6},{8,7},{9,8},{10,9},{11,1... | collective-permute-start | bytes 196616 | tf_op jit(solution)/shard_map/ppermute | solution.py:47
  17.8 41.4 %collective-permute-start = (f32[32,512]{1,0:T(8,128)S(1)}, f32[32,512]{1,0:T(8,128)S(1)}, u32[]{:S(2)}, u32[]{:S(2)}) collective-permute-start(f32[32,512]{1,0:T(8,128)S(1)} %get-tuple-element.256), channel_id=1, source_target_pairs={{0,1},{1,2},{2,3},{3,4},{4,5},{5,6},{6,7},{7,8},{8,9},{9,10},{10,1... | collective-permute-start | bytes 196616 | tf_op jit(solution)/shard_map/ppermute | solution.py:46
  20.4 13.6 %collective-permute-start.3 = (f32[3,512]{1,0:T(4,128)S(1)}, f32[3,512]{1,0:T(4,128)S(1)}, u32[]{:S(2)}, u32[]{:S(2)}) collective-permute-start(f32[3,512]{1,0:T(4,128)S(1)} %get-tuple-element.259), channel_id=1, source_target_pairs={{1,0},{2,1},{3,2},{4,3},{5,4},{6,5},{7,6},{8,7},{9,8},{10,9},{11,1... | collective-permute-start | bytes 18440 | tf_op jit(solution)/shard_map/ppermute | solution.py:47
  25.3 8.7 %collective-permute-start.2 = (f32[3,512]{1,0:T(4,128)S(1)}, f32[3,512]{1,0:T(4,128)S(1)}, u32[]{:S(2)}, u32[]{:S(2)}) collective-permute-start(f32[3,512]{1,0:T(4,128)S(1)} %get-tuple-element.258), channel_id=1, source_target_pairs={{0,1},{1,2},{2,3},{3,4},{4,5},{5,6},{6,7},{7,8},{8,9},{9,10},{10,1... | collective-permute-start | bytes 18440 | tf_op jit(solution)/shard_map/ppermute | solution.py:46
  33.2 26.0 %copy-start.1 = (f32[32,1024]{1,0:T(8,128)S(1)}, f32[32,1024]{1,0:T(8,128)}, u32[]{:S(2)}) copy-start(f32[32,1024]{1,0:T(8,128)} %param.14) | copy-start | bytes 393220
  34.7 7.5 %all-to-all-start.6 = ((f32[4,1,2048]{2,1,0:T(1,128)}), f32[4,1,2048]{2,1,0:T(1,128)S(1)}, u32[]{:S(2)}, u32[]{:S(2)}) async-start(f32[4,1,2048]{2,1,0:T(1,128)} %broadcast_in_dim.123), calls=%async_computation.6 | async-start | bytes 65536 | tf_op jit(solution)/shard_map/all_to_all | solution.py:23
  39.3 124.3 %copy-start.3 = (f32[4,8,64,64]{3,2,1,0:T(8,128)}, f32[4,8,64,64]{3,2,1,0:T(8,128)S(1)}, u32[]{:S(2)}) copy-start(f32[4,8,64,64]{3,2,1,0:T(8,128)S(1)} %multiply_reduce_fusion.6) | copy-start | bytes 1572868
  42.2 30.4 %all-to-all-start.4 = ((f32[64,1,192]{2,1,0:T(1,128)}), f32[64,1,192]{2,1,0:T(1,128)S(1)}, u32[]{:S(2)}, u32[]{:S(2)}) async-start(f32[64,1,192]{2,1,0:T(1,128)} %reshape.276), calls=%async_computation.4 | async-start | bytes 131072 | tf_op jit(solution)/shard_map/all_to_all | solution.py:23
  73.3 8.1 %all-to-all-start.3 = ((f32[4,4,2048]{2,1,0:T(4,128)}), f32[4,4,2048]{2,1,0:T(4,128)S(1)}, u32[]{:S(2)}, u32[]{:S(2)}) async-start(f32[4,4,2048]{2,1,0:T(4,128)} %broadcast_in_dim.117), calls=%async_computation.3 | async-start | bytes 262144 | tf_op jit(solution)/shard_map/all_to_all | solution.py:23
  88.8 79.7 %all-to-all-start.7 = ((f32[64,1,2048]{2,1,0:T(1,128)}), f32[64,1,2048]{2,1,0:T(1,128)S(1)}, u32[]{:S(2)}, u32[]{:S(2)}) async-start(f32[64,1,2048]{2,1,0:T(1,128)} %broadcast_in_dim.124), calls=%async_computation.7 | async-start | bytes 1048576 | tf_op jit(solution)/shard_map/all_to_all | solution.py:23
  175.2 0.7 copy-start.13
  175.5 1.7 copy-start.5
  175.9 2.4 copy-start.2
  187.0 8.4 %all-to-all-start.9 = ((f32[8,1,32]{2,1,0:T(1,128)}), f32[8,1,32]{2,1,0:T(1,128)S(1)}, u32[]{:S(2)}, u32[]{:S(2)}) async-start(f32[8,1,32]{2,1,0:T(1,128)} %broadcast_in_dim.127), calls=%async_computation.9 | async-start | bytes 8192 | tf_op jit(solution)/shard_map/all_to_all | solution.py:23
  196.0 28.1 %all-to-all-start.1 = ((f32[64,1,32]{2,1,0:T(1,128)}), f32[64,1,32]{2,1,0:T(1,128)S(1)}, u32[]{:S(2)}, u32[]{:S(2)}) async-start(f32[64,1,32]{2,1,0:T(1,128)} %broadcast_in_dim.111), calls=%async_computation.1 | async-start | bytes 65536 | tf_op jit(solution)/shard_map/all_to_all | solution.py:23
  224.7 17.8 %all-to-all-start.10 = ((f32[64,1,32]{2,1,0:T(1,128)}), f32[64,1,32]{2,1,0:T(1,128)S(1)}, u32[]{:S(2)}, u32[]{:S(2)}) async-start(f32[64,1,32]{2,1,0:T(1,128)} %broadcast_in_dim.128), calls=%async_computation.10 | async-start | bytes 65536 | tf_op jit(solution)/shard_map/all_to_all | solution.py:23
  270.9 19.1 %collective-permute-start.5 = (f32[32,512]{1,0:T(8,128)S(1)}, f32[32,512]{1,0:T(8,128)S(1)}, u32[]{:S(2)}, u32[]{:S(2)}) collective-permute-start(f32[32,512]{1,0:T(8,128)S(1)} %get-tuple-element.255), channel_id=1, source_target_pairs={{1,0},{2,1},{3,2},{4,3},{5,4},{6,5},{7,6},{8,7},{9,8},{10,9},{11,1... | collective-permute-start | bytes 196616 | tf_op jit(solution)/shard_map/ppermute | solution.py:47
  275.5 14.5 %collective-permute-start.4 = (f32[32,512]{1,0:T(8,128)S(1)}, f32[32,512]{1,0:T(8,128)S(1)}, u32[]{:S(2)}, u32[]{:S(2)}) collective-permute-start(f32[32,512]{1,0:T(8,128)S(1)} %get-tuple-element.254), channel_id=1, source_target_pairs={{0,1},{1,2},{2,3},{3,4},{4,5},{5,6},{6,7},{7,8},{8,9},{9,10},{10,1... | collective-permute-start | bytes 196616 | tf_op jit(solution)/shard_map/ppermute | solution.py:46
  278.3 7.7 %all-to-all-start.14 = ((f32[4,1,2048]{2,1,0:T(1,128)}), f32[4,1,2048]{2,1,0:T(1,128)S(1)}, u32[]{:S(2)}, u32[]{:S(2)}) async-start(f32[4,1,2048]{2,1,0:T(1,128)} %broadcast_in_dim.224), calls=%async_computation.14 | async-start | bytes 65536 | tf_op jit(solution)/shard_map/all_to_all | solution.py:23
  286.6 8.1 %all-to-all-start.13 = ((f32[4,4,2048]{2,1,0:T(4,128)}), f32[4,4,2048]{2,1,0:T(4,128)S(1)}, u32[]{:S(2)}, u32[]{:S(2)}) async-start(f32[4,4,2048]{2,1,0:T(4,128)} %broadcast_in_dim.222), calls=%async_computation.13 | async-start | bytes 262144 | tf_op jit(solution)/shard_map/all_to_all | solution.py:23
  295.8 78.5 %all-to-all-start.15 = ((f32[64,1,2048]{2,1,0:T(1,128)}), f32[64,1,2048]{2,1,0:T(1,128)S(1)}, u32[]{:S(2)}, u32[]{:S(2)}) async-start(f32[64,1,2048]{2,1,0:T(1,128)} %broadcast_in_dim.225), calls=%async_computation.15 | async-start | bytes 1048576 | tf_op jit(solution)/shard_map/all_to_all | solution.py:23
  370.8 1.2 copy-start.4
  382.9 1.4 copy-start.6
  382.9 2.3 copy-start.8
  383.0 2.4 copy-start.9
where the time goes:
time: 425 us; the launch traced here: 422 us
  starting transfers between devices  94.4 us (22%)
  blocking collectives  87.1 us (20%)
  matrix products  70.1 us (16%)
  waiting for transfers between devices  58.9 us (14%)
  loops' own time  55.5 us (13%)
  local copies, waits for them, and re-layouts  43.5 us (10%)
  other arithmetic  11.2 us (3%)
    all_to_all x8, blocking collectives, copy_for_each(): lax.all_to_all(jnp.broadcast_to(shard[None], (count, *shard.shape)), axis...  87.1 us
    all_to_all x11, starting transfers between devices, copy_for_each(): lax.all_to_all(jnp.broadcast_to(shard[None], (count, *shard.shape)), axis...  69.4 us
    all_to_all x11, waiting for transfers between devices, copy_for_each(): lax.all_to_all(jnp.broadcast_to(shard[None], (count, *shard.shape)), axis...  58.9 us
    another operation x2, loops' own time, near_field(): lax.map(one_position, jnp.arange(local_leaves + REACH, dtype=jnp.int32))  55.5 us
    dot_general x36, matrix products, one_position(): jnp.dot(other_values, kernel_tile.T, precision=HIGHEST)  38.8 us
    ppermute x3, starting transfers between devices, padded(): lax.ppermute(first, axis, [(b, a) for a, b in up])  19.2 us
    dot_general x24, matrix products, one_position(): jnp.dot(own_values, kernel_tile, precision=HIGHEST)  17.1 us
    broadcast_in_dim x22, local copies, waits for them, and re-layouts, copy_for_each(): jnp.broadcast_to(shard[None], (count, *shard.shape))  8.65 us
  transfers between devices with their start and end apart: 17, of which 8 were waited for; matrix products, arithmetic and copies ran while one was open for 25% of the time, Pallas kernels for 0%

commit v1 on v0

v1 whole, which is shorter than its diff:
```python
import functools

import jax
import jax.numpy as jnp
from jax import lax
from jax.experimental import pallas as pl
from jax.experimental.pallas import tpu as pltpu
from jax.sharding import PartitionSpec as P

LEAF = 256
RANK = 64
PROBES = 32
REACH = 2
OWN = 4
Z = 16
C = 2
WIN = OWN + 2 * REACH
SPAN = (2 * REACH + 1) * LEAF
HALO = REACH * LEAF
POINTS = OWN * LEAF
HIGHEST = lax.Precision.HIGHEST
MESH = pl.DeviceIdType.MESH
F32 = jnp.float32
BF16 = jnp.bfloat16
ROWS = 32

(
    HALO_PTS,
    HALO_VEC,
    SKEL_Y,
    COEF_Y,
    GROUP_XC,
    GROUP_Z,
    TERM_PLANE,
    FAR_Z,
    SQUARE_Y,
    BASE_Y,
    FAR_Y,
    TERM_XC,
    FAR_Z2,
    HALO_VEC2,
    COEF_Y2,
    FAR_Y2,
    DOT_PLANE,
    DOT_Z,
    DOT_PLANE2,
    DOT_Z2,
    EXCHANGES,
) = range(21)


def dot_nn(a, b):
    return jnp.dot(a, b, precision=HIGHEST, preferred_element_type=F32)


def dot_nt(a, b):
    return lax.dot_general(
        a, b, (((1,), (1,)), ((), ())), precision=HIGHEST, preferred_element_type=F32
    )


def dot_16(a, b):
    return jnp.dot(a, b, preferred_element_type=F32)


def three(values):
    first = values.astype(BF16).astype(F32)
    rest = values - first
    second = rest.astype(BF16).astype(F32)
    return first, second, rest - second


def matern(square, weight):
    square = 5.0 * square
    scaled = square * lax.rsqrt(jnp.maximum(square, 1e-30))
    return (weight + weight * scaled + (weight * (1.0 / 3.0)) * square) * jnp.exp(-scaled)


def distances(columns, rows):
    total = None
    for axis in range(3):
        spread = columns[:, axis : axis + 1] - rows[axis : axis + 1, :]
        total = spread * spread if total is None else total + spread * spread
    return total


def put_tile(high, low, where, tile):
    first = tile.astype(BF16)
    high[where] = first
    low[where] = (tile - first.astype(F32)).astype(BF16)


def kernel(
    X,
    Y,
    near_list,
    far_list,
    rhs,
    coords,
    group_list,
    basis,
    leaf_skel,
    leaf_transfer,
    device_transfer,
    group_skel,
    sol,
    res,
    vwin,
    wwin,
    split,
    pts,
    pts_t,
    near_hi,
    near_lo,
    skel,
    skel_t,
    coef,
    coef2,
    csplit,
    leaf_hi,
    leaf_lo,
    pay,
    pay_xc,
    pay_z,
    tgt,
    gmask,
    group_hi,
    group_lo,
    ee,
    ee2,
    term,
    term_in,
    zout,
    zin,
    zout2,
    zin2,
    square,
    base,
    base_in,
    gf,
    gf2,
    gfull,
    gfull2,
    next_term,
    next_in,
    part,
    dots,
    dot_plane,
    dots_z,
    dot_z,
    dots2,
    dot_plane2,
    dots_z2,
    dot_z2,
    send,
    recv,
):
    chunk = PROBES // Y
    plane = X * Y * C
    targets = Z * RANK
    leaf_at = lax.axis_index("leaf")
    y = lax.axis_index("sub")
    c = lax.rem(leaf_at, C)
    z = lax.rem(leaf_at // C, Z)
    x = leaf_at // (C * Z)
    node = leaf_at * Y + y
    nodes = X * Z * C * Y
    place = (x * Y + y) * C + c

    def at_node(q):
        return {"leaf": q // Y, "sub": lax.rem(q, Y)}

    def at_plane(p):
        px = p // (Y * C)
        return {"leaf": (px * Z + z) * C + lax.rem(p, C), "sub": lax.rem(p // C, Y)}

    def at_xc(p):
        return {"leaf": ((p // C) * Z + z) * C + lax.rem(p, C), "sub": y}

    def at_y(p):
        return {"leaf": leaf_at, "sub": p}

    def at_z(p):
        return {"leaf": (x * Z + p) * C + c, "sub": y}

    after = lax.rem(node + 1, nodes)
    before = lax.rem(node + nodes - 1, nodes)

    def put(src, dst, stage, device):
        pltpu.make_async_remote_copy(
            src_ref=src,
            dst_ref=dst,
            send_sem=send.at[stage],
            recv_sem=recv.at[stage],
            device_id=device,
            device_id_type=MESH,
        ).start()

    def to_others(mine, count, step):
        def body(k, carry):
            step(lax.rem(mine + k, count))
            return carry

        lax.fori_loop(1, count, body, 0)

    def arrived(ref, stage):
        pltpu.make_async_copy(ref, ref, recv.at[stage]).wait()

    def left(ref, stage):
        pltpu.make_async_copy(ref, ref, send.at[stage]).wait()

    barrier = pltpu.get_barrier_semaphore()

    def signal(device):
        pl.semaphore_signal(barrier, inc=1, device_id=device, device_id_type=MESH)

    to_others(z, Z, lambda p: signal(at_z(p)))
    to_others(place, plane, lambda p: signal(at_plane(p)))
    signal(at_node(after))
    signal(at_node(before))

    lane128 = lax.broadcasted_iota(jnp.int32, (1, 2 * RANK), 1)

    pay[...] = jnp.zeros_like(pay)
    pay[0:3, 0:RANK] = group_skel[...]
    pay[0:3, RANK : 2 * RANK] = group_skel[...]
    pay[3:4, 0:16] = group_list[...].astype(F32)

    on_core = (lax.broadcasted_iota(jnp.int32, (2 * RANK, 1), 0) // RANK == c).astype(F32)
    for i in range(OWN):
        down = dot_nn(leaf_transfer[i], device_transfer[0])
        e = dot_nn(down.T, basis[i])
        cols = slice(i * LEAF, (i + 1) * LEAF)
        ee[:, cols] = e
        ee2[:, cols] = jnp.concatenate([e, e], axis=0) * on_core
    own = slice(HALO, HALO + POINTS)
    vwin[:, own] = rhs[...]
    term[...] = dot_nt(rhs[...], ee2[...]).reshape(Y, chunk, 2 * RANK)
    square[y] = dot_nt(ee[...], ee2[...])

    def coefficients(vec, out):
        for i in range(OWN):
            out[:, i * RANK : (i + 1) * RANK] = dot_nt(
                vec[:, HALO + i * LEAF : HALO + (i + 1) * LEAF], basis[i]
            )

    coefficients(vwin, part)
    coef[y] = part[...]

    pts[:, own] = jnp.zeros((8, POINTS), F32)
    pts[0:3, own] = coords[...]
    pts_t[HALO : HALO + POINTS, :] = pts[:, own].T
    skel[y] = jnp.zeros((8, OWN * RANK), F32)
    skel[y, 0:3, :] = leaf_skel[...]

    def near_tile(i, o):
        target = node * OWN + i + o - REACH
        weight = jnp.float32(0.0)
        for s in range(2 * REACH + 1):
            weight = weight + jnp.where(near_list[i, s] == target, 1.0, 0.0)
        weight = jnp.where(target >= 0, weight, 0.0)
        rows = pts[:, HALO + i * LEAF : HALO + (i + 1) * LEAF]

        def body(r, carry):
            columns = pts_t[pl.ds((i + o) * LEAF + r * ROWS, ROWS), :]
            tile = matern(distances(columns, rows), weight)
            put_tile(near_hi, near_lo, (i, pl.ds(o * LEAF + r * ROWS, ROWS), slice(None)), tile)
            return carry

        lax.fori_loop(0, LEAF // ROWS, body, 0)

    for i in range(OWN):
        for o in range(2 * REACH + 1):
            if REACH <= i + o < REACH + OWN:
                near_tile(i, o)

    pl.semaphore_wait(barrier, Z - 1 + plane - 1 + 2)

    to_others(
        place,
        plane,
        lambda p: put(
            term.at[lax.rem(p // C, Y)], term_in.at[place], TERM_PLANE, at_plane(p)
        ),
    )
    to_others(z, Z, lambda p: put(pay, pay_z.at[z], GROUP_Z, at_z(p)))
    to_others(x * C + c, X * C, lambda p: put(pay, pay_xc.at[x * C + c], GROUP_XC, at_xc(p)))
    low, high = slice(HALO, 2 * HALO), slice(POINTS, POINTS + HALO)
    to_low, to_high = slice(0, HALO), slice(HALO + POINTS, 2 * HALO + POINTS)
    put(pts.at[:, high], pts.at[:, to_low], HALO_PTS, at_node(after))
    put(pts.at[:, low], pts.at[:, to_high], HALO_PTS, at_node(before))
    to_others(y, Y, lambda p: put(skel.at[y], skel.at[y], SKEL_Y, at_y(p)))
    put(vwin.at[:, high], vwin.at[:, to_low], HALO_VEC, at_node(after))
    put(vwin.at[:, low], vwin.at[:, to_high], HALO_VEC, at_node(before))
    to_others(y, Y, lambda p: put(coef.at[y], coef.at[y], COEF_Y, at_y(p)))
    to_others(y, Y, lambda p: put(square.at[y], square.at[y], SQUARE_Y, at_y(p)))
    pay_z[z] = pay[...]
    pay_xc[x * C + c] = pay[...]
    term_in[place] = term[y]

    both = slice(0, 2 * HALO)
    arrived(pts.at[:, both], HALO_PTS)
    pts_t[0:HALO, :] = pts[:, to_low].T
    pts_t[HALO + POINTS : 2 * HALO + POINTS, :] = pts[:, to_high].T
    for i in range(OWN):
        for o in range(2 * REACH + 1):
            if not REACH <= i + o < REACH + OWN:
                near_tile(i, o)

    leaf_lane = lax.broadcasted_iota(jnp.int32, (1, OWN * RANK), 1) // RANK
    listed = []
    for s in range(8):
        row = jnp.full((1, OWN * RANK), -1, jnp.int32)
        for i in range(OWN):
            row = jnp.where(leaf_lane == i, far_list[i, s], row)
        listed.append(row)
    arrived(skel.at[pl.ds(0, Y - 1)], SKEL_Y)
    group_first = leaf_at * Y * OWN
    own_skel = skel[y]
    for d in range(Y):
        skel_t[d * OWN * RANK : (d + 1) * OWN * RANK, :] = skel[d].T

    def leaf_tile(m, carry):
        mask = jnp.zeros((1, OWN * RANK), F32)
        for row in listed:
            mask = mask + jnp.where(row == group_first + m, 1.0, 0.0)
        for r in range(RANK // ROWS):
            at = pl.ds(m * RANK + r * ROWS, ROWS)
            tile = matern(distances(skel_t[at, :], own_skel), mask)
            put_tile(leaf_hi, leaf_lo, (at, slice(None)), tile)
        return carry

    lax.fori_loop(0, Y * OWN, leaf_tile, 0)

    def three_of(vec):
        first, second, third = three(vec)
        split[0:PROBES, :] = first.astype(BF16)
        split[PROBES : 2 * PROBES, :] = second.astype(BF16)
        split[2 * PROBES : 3 * PROBES, :] = third.astype(BF16)

    def near_of(i):
        cols = slice(i * LEAF, i * LEAF + SPAN)
        a = dot_16(split[:, cols], near_hi[i])
        b = dot_16(split[0 : 2 * PROBES, cols], near_lo[i])
        return (
            (a[2 * PROBES :] + b[PROBES:])
            + (a[PROBES : 2 * PROBES] + b[0:PROBES])
            + a[0:PROBES]
        )

    def leaf_far(coefs):
        for d in range(Y):
            cols = slice(d * OWN * RANK, (d + 1) * OWN * RANK)
            first, second, third = three(coefs[d])
            csplit[0:PROBES, cols] = first.astype(BF16)
            csplit[PROBES : 2 * PROBES, cols] = second.astype(BF16)
            csplit[2 * PROBES : 3 * PROBES, cols] = third.astype(BF16)
        a = dot_16(csplit[...], leaf_hi[...])
        b = dot_16(csplit[0 : 2 * PROBES, :], leaf_lo[...])
        return (
            (a[2 * PROBES :] + b[PROBES:])
            + (a[PROBES : 2 * PROBES] + b[0:PROBES])
            + a[0:PROBES]
        )

    def local_image(vec, coefs, out):
        part[...] = leaf_far(coefs)
        for i in range(OWN):
            cols = slice(HALO + i * LEAF, HALO + (i + 1) * LEAF)
            far = dot_nn(part[:, i * RANK : (i + 1) * RANK], basis[i])
            out[:, cols] = vec[:, cols] + near_of(i) + far

    arrived(vwin.at[:, both], HALO_VEC)
    three_of(vwin[...])
    arrived(coef.at[pl.ds(0, Y - 1)], COEF_Y)
    local_image(vwin, coef, wwin)

    base[...] = dot_nt(wwin[:, own], ee2[...]).reshape(Y, chunk, 2 * RANK)
    to_others(y, Y, lambda p: put(base.at[p], base_in.at[y], BASE_Y, at_y(p)))
    base_in[y] = base[y]

    arrived(pay_xc.at[pl.ds(0, X * C - 1)], GROUP_XC)
    arrived(pay_z.at[pl.ds(0, Z - 1)], GROUP_Z)
    for k in range(Z // 2):
        tgt[:, k * 128 : (k + 1) * 128] = jnp.where(lane128 < RANK, pay_z[2 * k], pay_z[2 * k + 1])
    ids = lax.broadcasted_iota(jnp.int32, (1, targets), 1) // RANK
    ids = ((x * Z + ids) * C + c).astype(F32)

    def group_tile(h, carry):
        turned = pay_xc[h].T
        mask = jnp.sum(jnp.where(turned[0:16, 3:4] == ids, 1.0, 0.0), axis=0, keepdims=True)
        gmask[...] = mask
        for k in range(targets // 128):
            lanes = slice(k * 128, (k + 1) * 128)
            tile = matern(distances(turned[0:RANK, :], tgt[:, lanes]), gmask[:, lanes])
            put_tile(group_hi, group_lo, (pl.ds(h * RANK, RANK), lanes), tile)
        return carry

    lax.fori_loop(0, X * C, group_tile, 0)

    def group_far(sources, out):
        terms = [three(s) for s in sources]
        stacked = [jnp.concatenate([t[k] for t in terms], axis=1) for k in range(3)]
        stacked.append(jnp.zeros_like(stacked[0]))
        stacked = jnp.concatenate(stacked, axis=0).astype(BF16)
        a = dot_16(stacked, group_hi[...])
        b = dot_16(stacked, group_lo[...])
        a = [a[k * chunk : (k + 1) * chunk] for k in range(3)]
        b = [b[k * chunk : (k + 1) * chunk] for k in range(2)]
        total = (a[2] + b[1]) + (a[1] + b[0]) + a[0]
        for k in range(Z):
            out[k] = total[:, k * RANK : (k + 1) * RANK]

    def summed(ref, count, first=0):
        total = ref[first]
        for k in range(1, count):
            total = total + ref[first + k]
        return total

    arrived(term_in.at[pl.ds(0, plane - 1)], TERM_PLANE)
    group_far([summed(term_in, Y * C, k * Y * C) for k in range(X)], zout)
    to_others(z, Z, lambda p: put(zout.at[p], zin.at[z], FAR_Z, at_z(p)))
    zin[z] = zout[z]
    first_term = summed(term_in, Y * C, x * Y * C) * (lane128 // RANK == c).astype(F32)

    arrived(base_in.at[pl.ds(0, Y - 1)], BASE_Y)
    base_sum = summed(base_in, Y)
    arrived(square.at[pl.ds(0, Y - 1)], SQUARE_Y)
    square_sum = summed(square, Y)

    row_of = lax.broadcasted_iota(jnp.int32, (PROBES, 1), 0)
    own_rows = (row_of // chunk == y).astype(F32)

    def lanes_of(a, b, width=POINTS):
        total = a[:, 0:128] * b[:, 0:128]
        for k in range(1, width // 128):
            cols = slice(k * 128, (k + 1) * 128)
            total = total + a[:, cols] * b[:, cols]
        return total

    ones = jnp.ones((8, 128), F32)

    def total_lanes(parts):
        parts = parts + [jnp.zeros((PROBES, 128), F32)] * (4 - len(parts))
        return dot_nt(ones, jnp.concatenate(parts, axis=0))[0:1, :]

    def all_rows(block):
        return jnp.concatenate([block] * Y, axis=0)

    rhs_now = rhs[...]
    rr_lanes = lanes_of(rhs_now, rhs_now)
    curve_lanes = lanes_of(rhs_now, wwin[:, own])

    arrived(zin.at[pl.ds(0, Z - 1)], FAR_Z)
    got = summed(zin, Z)
    gf[...] = got
    following = base_sum + dot_nn(got, square_sum)
    next_term[...] = following
    to_others(
        x * C + c, X * C, lambda p: put(next_term, next_in.at[x * C + c], TERM_XC, at_xc(p))
    )
    to_others(y, Y, lambda p: put(gf, gfull.at[y], FAR_Y, at_y(p)))
    next_in[x * C + c] = following
    gfull[y] = got
    twice = jnp.concatenate([got, got], axis=1)
    dots[...] = total_lanes([rr_lanes, curve_lanes + own_rows * all_rows(first_term * twice)])
    to_others(place, plane, lambda p: put(dots, dot_plane.at[place], DOT_PLANE, at_plane(p)))
    dot_plane[place] = dots[...]

    arrived(gfull.at[pl.ds(0, Y - 1)], FAR_Y)
    wwin[:, own] = wwin[:, own] + dot_nn(gfull[...].reshape(PROBES, RANK), ee[...])
    put(wwin.at[:, high], wwin.at[:, to_low], HALO_VEC2, at_node(after))
    put(wwin.at[:, low], wwin.at[:, to_high], HALO_VEC2, at_node(before))
    coefficients(wwin, part)
    coef2[y] = part[...]
    to_others(y, Y, lambda p: put(coef2.at[y], coef2.at[y], COEF_Y2, at_y(p)))

    arrived(next_in.at[pl.ds(0, X * C - 1)], TERM_XC)
    group_far([summed(next_in, C, k * C) for k in range(X)], zout2)
    to_others(z, Z, lambda p: put(zout2.at[p], zin2.at[z], FAR_Z2, at_z(p)))
    zin2[z] = zout2[z]

    arrived(dot_plane.at[pl.ds(0, plane - 1)], DOT_PLANE)
    plane_sum = jnp.sum(dot_plane[...], axis=0)
    dots_z[...] = plane_sum
    to_others(z, Z, lambda p: put(dots_z, dot_z.at[z], DOT_Z, at_z(p)))
    dot_z[z] = plane_sum

    arrived(wwin.at[:, both], HALO_VEC2)
    three_of(wwin[...])
    arrived(coef2.at[pl.ds(0, Y - 1)], COEF_Y2)
    left(vwin.at[:, both], HALO_VEC)
    local_image(wwin, coef2, vwin)

    lane_of = lax.broadcasted_iota(jnp.int32, (PROBES, 128), 1)

    def column(row, k):
        hit = (lane_of == row_of + k * PROBES).astype(F32)
        return jnp.sum(hit * row, axis=1, keepdims=True)

    arrived(zin2.at[pl.ds(0, Z - 1)], FAR_Z2)
    got2 = summed(zin2, Z)
    gf2[...] = got2
    to_others(y, Y, lambda p: put(gf2, gfull2.at[y], FAR_Y2, at_y(p)))
    gfull2[y] = got2
    twice2 = jnp.concatenate([got2, got2], axis=1)
    first_far = own_rows * all_rows(first_term * twice2)
    second_far = own_rows * all_rows(following * twice2)

    arrived(dot_z.at[pl.ds(0, Z - 1)], DOT_Z)
    sums = jnp.sum(dot_z[...], axis=0)
    rr0 = column(sums, 0)
    curve0 = column(sums, 1)
    step0 = rr0 / curve0
    image1 = wwin[:, own]
    image2 = vwin[:, own]
    residual1 = rhs_now - step0 * image1
    turned_lanes = lanes_of(residual1, image1)
    dots2[...] = total_lanes(
        [
            lanes_of(residual1, residual1),
            turned_lanes - step0 * (lanes_of(residual1, image2) + first_far - step0 * second_far),
            turned_lanes - step0 * (lanes_of(rhs_now, image2) + first_far),
        ]
    )
    to_others(place, plane, lambda p: put(dots2, dot_plane2.at[place], DOT_PLANE2, at_plane(p)))
    dot_plane2[place] = dots2[...]

    arrived(gfull2.at[pl.ds(0, Y - 1)], FAR_Y2)
    image2 = image2 + dot_nn(gfull2[...].reshape(PROBES, RANK), ee[...])
    turned1 = image1 - step0 * image2

    arrived(dot_plane2.at[pl.ds(0, plane - 1)], DOT_PLANE2)
    plane_sum2 = jnp.sum(dot_plane2[...], axis=0)
    dots_z2[...] = plane_sum2
    to_others(z, Z, lambda p: put(dots_z2, dot_z2.at[z], DOT_Z2, at_z(p)))
    dot_z2[z] = plane_sum2
    arrived(dot_z2.at[pl.ds(0, Z - 1)], DOT_Z2)
    sums2 = jnp.sum(dot_z2[...], axis=0)
    rr1 = column(sums2, 0)
    ratio = rr1 / rr0
    curve1 = column(sums2, 1) + ratio * (column(sums2, 2) + curve0) + ratio * ratio * curve0
    step1 = rr1 / curve1
    direction1 = residual1 + ratio * rhs_now
    sol[...] = step0 * rhs_now + step1 * direction1
    res[...] = residual1 - step1 * (turned1 + ratio * image1)

    left(pts.at[:, both], HALO_PTS)
    left(wwin.at[:, both], HALO_VEC2)
    for ref, stage in (
        (skel, SKEL_Y),
        (coef, COEF_Y),
        (coef2, COEF_Y2),
        (square, SQUARE_Y),
        (base_in, BASE_Y),
        (gfull, FAR_Y),
        (gfull2, FAR_Y2),
    ):
        left(ref.at[pl.ds(0, Y - 1)], stage)
    for ref, stage in ((pay_z, GROUP_Z), (zin, FAR_Z), (zin2, FAR_Z2), (dot_z, DOT_Z), (dot_z2, DOT_Z2)):
        left(ref.at[pl.ds(0, Z - 1)], stage)
    left(pay_xc.at[pl.ds(0, X * C - 1)], GROUP_XC)
    left(term_in.at[pl.ds(0, plane - 1)], TERM_PLANE)
    left(next_in.at[pl.ds(0, X * C - 1)], TERM_XC)
    left(dot_plane.at[pl.ds(0, plane - 1)], DOT_PLANE)
    left(dot_plane2.at[pl.ds(0, plane - 1)], DOT_PLANE2)


def shards(X, Y, rhs, coords, near_list, far_list, group_list, basis, skel, transfer, device, group):
    chunk = PROBES // Y
    plane = X * Y * C
    targets = Z * RANK
    sources = X * C * RANK
    window = WIN * LEAF
    own_rank = OWN * RANK

    def f32(*shape):
        return pltpu.VMEM(shape, F32)

    def b16(*shape):
        return pltpu.VMEM(shape, BF16)

    vmem = pl.BlockSpec(memory_space=pltpu.VMEM)
    smem = pl.BlockSpec(memory_space=pltpu.SMEM)
    block = jax.ShapeDtypeStruct((PROBES, POINTS), F32)
    return pl.pallas_call(
        functools.partial(kernel, X, Y),
        out_shape=(block, block),
        in_specs=[smem, smem] + [vmem] * 8,
        out_specs=(vmem, vmem),
        scratch_shapes=[
            f32(PROBES, window),
            f32(PROBES, window),
            b16(3 * PROBES, window),
            f32(8, window),
            f32(window, 8),
            b16(OWN, SPAN, LEAF),
            b16(OWN, SPAN, LEAF),
            f32(Y, 8, own_rank),
            f32(Y * own_rank, 8),
            f32(Y, PROBES, own_rank),
            f32(Y, PROBES, own_rank),
            b16(3 * PROBES, Y * own_rank),
            b16(Y * own_rank, own_rank),
            b16(Y * own_rank, own_rank),
            f32(8, 128),
            f32(X * C, 8, 128),
            f32(Z, 8, 128),
            f32(8, targets),
            f32(1, targets),
            b16(sources, targets),
            b16(sources, targets),
            f32(RANK, POINTS),
            f32(2 * RANK, POINTS),
            f32(Y, chunk, 2 * RANK),
            f32(plane, chunk, 2 * RANK),
            f32(Z, chunk, RANK),
            f32(Z, chunk, RANK),
            f32(Z, chunk, RANK),
            f32(Z, chunk, RANK),
            f32(Y, RANK, 2 * RANK),
            f32(Y, chunk, 2 * RANK),
            f32(Y, chunk, 2 * RANK),
            f32(chunk, RANK),
            f32(chunk, RANK),
            f32(Y, chunk, RANK),
            f32(Y, chunk, RANK),
            f32(chunk, 2 * RANK),
            f32(X * C, chunk, 2 * RANK),
            f32(PROBES, own_rank),
            f32(1, 128),
            f32(plane, 1, 128),
            f32(1, 128),
            f32(Z, 1, 128),
            f32(1, 128),
            f32(plane, 1, 128),
            f32(1, 128),
            f32(Z, 1, 128),
            pltpu.SemaphoreType.DMA((EXCHANGES,)),
            pltpu.SemaphoreType.DMA((EXCHANGES,)),
        ],
        compiler_params=pltpu.CompilerParams(
            collective_id=0, has_side_effects=True, vmem_limit_bytes=40 * 2**20
        ),
    )(near_list, far_list, rhs, coords, group_list, basis, skel, transfer, device, group)


def solution(mesh):
    both = ("leaf", "sub")
    X, Y = mesh.shape["leaf"] // (Z * C), mesh.shape["sub"]
    in_specs = (
        P(None, both),
        P(None, both),
        P(both, None),
        P(both, None),
        P("leaf", None),
        P(both, None, None),
        P(None, both),
        P(both, None, None),
        P(both, None, None),
        P(None, "leaf"),
    )
    out_specs = (P(None, both), P(None, both))
    return jax.shard_map(
        functools.partial(shards, X, Y),
        mesh=mesh,
        in_specs=in_specs,
        out_specs=out_specs,
        check_vma=False,
    )
```

time: 425 us -> 91 us (0.21)
  starting transfers between devices: 94.4 us -> 0 us
  blocking collectives: 87.1 us -> 0 us
  Pallas kernels: 0 us -> 81 us
  matrix products: 70.1 us -> 0 us
  waiting for transfers between devices: 58.9 us -> 0 us
  loops' own time: 55.5 us -> 0 us
  local copies, waits for them, and re-layouts: 43.5 us -> 8.92 us
  other arithmetic: 11.2 us -> 0 us
    all_to_all x8 -> x0, blocking collectives: 87.1 us -> none  [copy_for_each(): lax.all_to_all(jnp.broadcast_to(shard[None], (count, *shard.shape)), axis...]
    pallas_call x0 -> x1, Pallas kernels: none -> 81 us  [shards(): pl.pallas_call(functools.partial(kernel, X, Y), out_shape=(block, block),...]
    dot_general x80 -> x0, matrix products: 70.1 us -> none  [the longest x36 38.8 us: one_position(): jnp.dot(other_values, kernel_tile.T, precision=HIGHEST)]
    all_to_all x11 -> x0, starting transfers between devices: 69.4 us -> none  [copy_for_each(): lax.all_to_all(jnp.broadcast_to(shard[None], (count, *shard.shape)), axis...]
    all_to_all x11 -> x0, waiting for transfers between devices: 58.9 us -> none  [copy_for_each(): lax.all_to_all(jnp.broadcast_to(shard[None], (count, *shard.shape)), axis...]
    another operation x2 -> x0, loops' own time: 55.5 us -> none  [near_field(): lax.map(one_position, jnp.arange(local_leaves + REACH, dtype=jnp.int32))]
    ppermute x6 -> x0, starting transfers between devices: 25 us -> none  [the longest x3 19.2 us: padded(): lax.ppermute(first, axis, [(b, a) for a, b in up])]
    slice x27 -> x0, local copies, waits for them, and re-layouts: 16.2 us -> none  [the longest x12 7.61 us: one_position(): own_weights[REACH + offset]]
  transfers between devices with their start and end apart: 17 -> 0, of which waited for: 8 -> 0; matrix products, arithmetic and copies ran while one was open for 25% -> 0% of each run, Pallas kernels for 0% -> 0%
where the time goes in v1:
time: 91 us; the launch traced here: 90.6 us
  Pallas kernels  81 us (89%)
  local copies, waits for them, and re-layouts  8.92 us (10%)
    pallas_call x1, Pallas kernels, shards(): pl.pallas_call(functools.partial(kernel, X, Y), out_shape=(block, block),...  81 us
    unnamed x22, local copies, waits for them, and re-layouts  8.92 us

profile of v1, /device:TPU:1, one launch (start us, length us, event | category | flops | bytes accessed | tf_op | source)
XLA Modules:
  0.0 90.6 jit_solution(2902276381070274607)
XLA Ops:
  0.6 0.0 copy-start
  0.6 0.9 %copy-done = f32[4,64,256]{2,1,0:T(8,128)S(1)} copy-done((f32[4,64,256]{2,1,0:T(8,128)S(1)}, f32[4,64,256]{2,1,0:T(8,128)}, u32[]{:S(2)}) %copy-start) | copy-done | bytes 262168
  1.6 0.0 copy-start.1
  1.6 0.9 copy-done.1
  2.5 0.0 copy-start.2
  2.5 0.9 copy-done.2
  3.4 0.0 copy-start.3
  3.4 0.8 copy-done.3
  4.2 0.0 copy-start.4
  4.2 0.7 copy-done.4
  4.9 0.0 copy-start.5
  4.9 0.7 copy-done.5
  5.6 0.0 copy-start.6
  5.6 0.7 copy-done.6
  6.2 0.0 copy-start.7
  6.2 0.7 copy-done.7
  6.9 0.0 copy-start.8
  6.9 0.7 copy-done.8
  7.6 0.0 copy-start.9
  7.6 0.7 copy-done.9
  8.3 81.0 %shard_map.113 = (f32[32,1024]{1,0:T(8,128)S(1)}, f32[32,1024]{1,0:T(8,128)S(1)}) custom-call(s32[4,5]{1,0:T(4,128)S(1)} %copy-done.6, s32[4,8]{1,0:T(4,128)S(1)} %copy-done.7, f32[32,1024]{1,0:T(8,128)S(1)} %copy-done.1, f32[3,1024]{1,0:T(4,128)S(1)} %copy-done.4, s32[1,16]{1,0:T(1,128)S(1)} %copy-done.9, f32[4,64,256]{2,1,0:T(8,128)S(1)} %copy-done, ...), custom_call_target="tpu_custom_call" | custom-call | tf_op jit(solution)/shard_map/pallas_call | solution.py:586
  89.3 0.7 copy.14
  89.9 0.7 copy.15
Async XLA Ops:
  0.6 1.0 %copy-start = (f32[4,64,256]{2,1,0:T(8,128)S(1)}, f32[4,64,256]{2,1,0:T(8,128)}, u32[]{:S(2)}) copy-start(f32[4,64,256]{2,1,0:T(8,128)} %basis.1) | copy-start | bytes 786436
  1.6 0.9 copy-start.1
  2.5 0.9 copy-start.2
  3.4 0.8 copy-start.3
  4.2 0.7 copy-start.4
  4.9 0.7 copy-start.5
  5.6 0.7 copy-start.6
  6.2 0.7 copy-start.7
  6.9 0.7 copy-start.8
  7.6 0.7 copy-start.9
